TPU v7x, 512 devices: a whole 4x8x8 slice. The times are simulated.
512 devices in a mesh: side: 4 (over z_lo, core), grp: 8 (over y), tp: 16 (over x, z_hi).
Axes of the slice: x: 4, y: 8, z: 8 (z_hi: 4, z_lo: 2; z = z_hi * 2 + z_lo), core: 2. Of those that a mesh axis runs over, the one named last changes fastest.
Arguments:
- resident_kv: bfloat16 [1024, 256, 2048], P(('side', 'grp', 'tp')), may hold values from -32 to 32
- resident_query: bfloat16 [1024, 16384], P(('side', 'grp'), 'tp'), may hold values from -32 to 32
- resident_new: bfloat16 [1024, 2048], P(('side', 'grp', 'tp')), may hold values from -9 to 9
- lengths: int32 [1024], P(('side', 'grp', 'tp')), may hold values from 2 to 256
- fresh_kv: bfloat16 [4096, 16, 2048], P(('side', 'grp', 'tp')), may hold values from -32 to 32
- handed_query: bfloat16 [32, 16, 8, 2, 16384], P(('side', 'grp'), None, None, None, 'tp'), may hold values from -32 to 32
- fresh_new: bfloat16 [4096, 2048], P(('side', 'grp', 'tp')), may hold values from -9 to 9
- matching: int32 [4096, 1], P(('side', 'grp', 'tp')), may hold values from 0 to 7; in each aligned block of 8 rows (0 to 7, 8 to 15, ...) at most 2 rows name the same one
Outputs:
- resident_out: bfloat16 [1024, 16384], P(('side', 'grp'), 'tp')
- handed_out: bfloat16 [32, 16, 8, 2, 16384], P(('side', 'grp'), None, None, None, 'tp')
- handed_cache_out: bfloat16 [32, 16, 8, 2, 16, 2048], P(('side', 'grp'), 'tp')
Inputs may be any that keep to these rules, and one draw needn't show every extreme that they name: `matching`: within each device's 8 requests no decode group is named more than 2 times.
All inputs are finite; a program needn't handle non-finite values.
Results may differ from a plain program's by a relative error of at most 0.0026.
Values may be sent and summed in bfloat16 or wider, within the bound.
A program may use at most 64 MiB of HBM per device.

v0:
```python
import math

import jax
import jax.numpy as jnp
from jax import lax
from jax.sharding import PartitionSpec as P

QH = 128
KVH = 8
HD = 128


NEG_FILL = -1e30


def from_behind(array, axis, by):
    devices = lax.axis_size(axis)
    return lax.ppermute(array, axis, [(i, (i + by) % devices) for i in range(devices)])


def attend(queries, cache, new_pair, valid):
    count, length = (cache.shape[0], cache.shape[1])
    group = QH // KVH
    scale = 1.0 / math.sqrt(HD)
    query_heads = queries.reshape(count, KVH, group, HD)
    keys = cache[:, :, : KVH * HD].reshape(count, length, KVH, HD)
    values = cache[:, :, KVH * HD :].reshape(count, length, KVH, HD)
    scores = (
        jnp.einsum("bhgd,blhd->bhgl", query_heads, keys, preferred_element_type=jnp.float32) * scale
    )
    scores = jnp.where(valid[:, None, None, :], scores, NEG_FILL)
    new_keys = new_pair[:, : KVH * HD].reshape(count, KVH, HD)
    new_values = new_pair[:, KVH * HD :].reshape(count, KVH, HD).astype(jnp.float32)
    new_scores = (
        jnp.einsum("bhgd,bhd->bhg", query_heads, new_keys, preferred_element_type=jnp.float32)
        * scale
    )
    top = jnp.maximum(jnp.max(scores, axis=-1), new_scores)
    probs = jnp.where(valid[:, None, None, :], jnp.exp(scores - top[..., None]), 0.0)
    new_probs = jnp.exp(new_scores - top)
    totals = jnp.sum(probs, axis=-1) + new_probs
    weights = probs.astype(jnp.bfloat16)
    numer = jnp.einsum("bhgl,blhd->bhgd", weights, values, preferred_element_type=jnp.float32)
    new_weights = lax.optimization_barrier(new_probs.astype(jnp.bfloat16)).astype(jnp.float32)
    numer = numer + new_weights[..., None] * new_values[:, :, None, :]
    return (numer / totals[..., None]).reshape(count, QH * HD).astype(jnp.bfloat16)


def body(
    resident_kv, resident_query, resident_new, lengths, fresh_kv, handed_query, fresh_new, matching
):
    tp_count = lax.axis_size("tp")
    group_count = lax.axis_size("grp")
    side_count = lax.axis_size("side")
    res_len = resident_kv.shape[1]
    requests, fresh_len = (fresh_kv.shape[0], fresh_kv.shape[1])
    capacity = max(2, 2 * requests // group_count)
    slots = group_count * capacity
    target = matching[:, 0]
    order = jnp.arange(requests, dtype=jnp.int32)
    before = (target[:, None] == target[None, :]) & (order[:, None] < order[None, :])
    rank = jnp.sum(before.astype(jnp.int32), axis=0)
    place = target * capacity + rank
    select = (jnp.arange(slots, dtype=jnp.int32)[:, None] == place[None, :]).astype(jnp.bfloat16)

    def pack(values):
        flat = values.reshape(requests, -1)
        packed = jnp.dot(select, flat, preferred_element_type=jnp.float32).astype(jnp.bfloat16)
        return packed.reshape((group_count, capacity) + values.shape[1:])

    occupied = (
        jnp.sum(select.astype(jnp.float32), axis=1)
        .astype(jnp.bfloat16)
        .reshape(group_count, capacity)
    )
    outgoing = (pack(fresh_kv), pack(fresh_new), occupied)
    routed = (
        lax.all_to_all(outgoing[0], "grp", split_axis=0, concat_axis=0, tiled=True),
        lax.all_to_all(outgoing[1], "grp", split_axis=0, concat_axis=0, tiled=True),
        lax.all_to_all(outgoing[2], "grp", split_axis=0, concat_axis=0, tiled=True),
    )
    arrived = from_behind((routed[0], routed[1], routed[2]), "side", side_count // 2)
    full_handed_query = lax.all_to_all(handed_query, "tp", split_axis=1, concat_axis=4, tiled=True)
    full_query = lax.all_to_all(resident_query, "tp", split_axis=0, concat_axis=1, tiled=True)
    positions = jnp.arange(res_len, dtype=jnp.int32)
    valid_res = positions[None, :] < lengths[:, None]
    res_out = attend(full_query, resident_kv, resident_new, valid_res)
    resident_out = lax.all_to_all(res_out, "tp", split_axis=1, concat_axis=0, tiled=True)
    handed_kv = arrived[0].reshape(slots, fresh_len, 2 * KVH * HD)
    handed_new = arrived[1].reshape(slots, 2 * KVH * HD)
    handed_flag = arrived[2].reshape(slots, 1)
    slot_query = full_handed_query.reshape(slots, QH * HD)
    valid_hand = jnp.ones((slots, fresh_len), dtype=bool)
    hand_out = attend(slot_query, handed_kv, handed_new, valid_hand) * handed_flag
    hand_out = hand_out.reshape(1, group_count, capacity, QH * HD)
    handed = lax.all_to_all(hand_out, "tp", split_axis=3, concat_axis=0, tiled=True)
    handed_out = handed.reshape(1, tp_count, group_count, capacity, QH * HD // tp_count)
    handed_cache_out = handed_kv.reshape(1, 1, group_count, capacity, fresh_len, 2 * KVH * HD)
    return (resident_out, handed_out, handed_cache_out)


def solution(mesh):
    return jax.shard_map(
        body,
        mesh=mesh,
        in_specs=(
            P(("side", "grp", "tp"), None, None),
            P(("side", "grp"), "tp"),
            P(("side", "grp", "tp"), None),
            P(("side", "grp", "tp")),
            P(("side", "grp", "tp"), None, None),
            P(("side", "grp"), None, None, None, "tp"),
            P(("side", "grp", "tp"), None),
            P(("side", "grp", "tp"), None),
        ),
        out_specs=(
            P(("side", "grp"), "tp"),
            P(("side", "grp"), None, None, None, "tp"),
            P(("side", "grp"), "tp", None, None, None, None),
        ),
        check_vma=False,
    )
```

profile of v0, /device:TPU:1, one launch (start us, length us, event | category | flops | bytes accessed | tf_op | source)
XLA Modules:
  0.0 199.2 jit_solution(14932605207243611539)
XLA Ops:
  0.7 0.8 convert_reduce_fusion
  2.9 7.7 %all-to-all-start.5 = ((bf16[8,1,2]{2,1,0:T(2,128)(2,1)}), bf16[8,1,2]{2,1,0:T(2,128)(2,1)S(1)}, u32[]{:S(2)}, u32[]{:S(2)}) async-start(bf16[8,1,2]{2,1,0:T(2,128)(2,1)} %all_to_all.77), calls=%async_computation.5 | async-start | bytes 8192 | tf_op jit(solution)/shard_map/all_to_all | solution.py:80
  10.8 0.7 reshape.140
  11.5 5.5 %all-to-all-done.5 = bf16[8,1,2]{2,1,0:T(2,128)(2,1)S(1)} async-done(((bf16[8,1,2]{2,1,0:T(2,128)(2,1)}), bf16[8,1,2]{2,1,0:T(2,128)(2,1)S(1)}, u32[]{:S(2)}, u32[]{:S(2)}) %all-to-all-start.5) | async-done | bytes 64 | tf_op jit(solution)/shard_map/all_to_all | solution.py:80
  17.0 3.4 %all-to-all-start.4 = ((bf16[8,2,2048]{2,1,0:T(2,128)(2,1)}), bf16[8,2,2048]{2,1,0:T(2,128)(2,1)S(1)}, u32[]{:S(2)}, u32[]{:S(2)}) async-start(bf16[8,2,2048]{2,1,0:T(2,128)(2,1)} %reshape.140), calls=%async_computation.4 | async-start | bytes 131072 | tf_op jit(solution)/shard_map/all_to_all | solution.py:79
  20.4 1.3 copy.75
  21.7 1.5 all_to_all.60
  23.2 4.3 %all-to-all-done.4 = bf16[8,2,2048]{2,1,0:T(2,128)(2,1)S(1)} async-done(((bf16[8,2,2048]{2,1,0:T(2,128)(2,1)}), bf16[8,2,2048]{2,1,0:T(2,128)(2,1)S(1)}, u32[]{:S(2)}, u32[]{:S(2)}) %all-to-all-start.4) | async-done | bytes 65568 | tf_op jit(solution)/shard_map/all_to_all | solution.py:79
  27.5 12.6 %all-to-all-start = ((bf16[16,2,1024]{2,1,0:T(2,128)(2,1)}), bf16[16,2,1024]{2,1,0:T(2,128)(2,1)S(1)}, u32[]{:S(2)}, u32[]{:S(2)}) async-start(bf16[16,2,1024]{2,1,0:T(2,128)(2,1)} %all_to_all.60), calls=%async_computation | async-start | bytes 131072 | tf_op jit(solution)/shard_map/all_to_all | solution.py:84
  40.7 1.5 copy.76
  42.2 7.1 %all-to-all-done = bf16[16,2,1024]{2,1,0:T(2,128)(2,1)S(1)} async-done(((bf16[16,2,1024]{2,1,0:T(2,128)(2,1)}), bf16[16,2,1024]{2,1,0:T(2,128)(2,1)S(1)}, u32[]{:S(2)}, u32[]{:S(2)}) %all-to-all-start) | async-done | bytes 65568 | tf_op jit(solution)/shard_map/all_to_all | solution.py:84
  49.3 4.2 %all-to-all-start.2 = ((bf16[8,2,16,2048]{3,2,1,0:T(8,128)(2,1)}), bf16[8,2,16,2048]{3,2,1,0:T(8,128)(2,1)}, u32[]{:S(2)}, u32[]{:S(2)}) async-start(bf16[8,2,16,2048]{3,2,1,0:T(8,128)(2,1)} %bitcast.32), calls=%async_computation.2 | async-start | bytes 2097152 | tf_op jit(solution)/shard_map/all_to_all | solution.py:78
  53.6 1.7 fusion.30
  56.6 2.9 %collective-permute-start.2 = (bf16[8,2]{0,1:T(2,128)(2,1)S(1)}, bf16[8,2]{0,1:T(2,128)(2,1)S(1)}, u32[]{:S(2)}, u32[]{:S(2)}) collective-permute-start(bf16[8,2]{0,1:T(2,128)(2,1)S(1)} %bitcast.86), channel_id=1, source_target_pairs={{0,256},{128,384},{256,0},{384,128},{1,257},{129,385},{257,1},{385... | collective-permute-start | bytes 104 | tf_op jit(solution)/shard_map/ppermute | solution.py:18
  59.5 2.4 %collective-permute-start.1 = (bf16[8,2,2048]{2,1,0:T(2,128)(2,1)S(1)}, bf16[8,2,2048]{2,1,0:T(2,128)(2,1)S(1)}, u32[]{:S(2)}, u32[]{:S(2)}) collective-permute-start(bf16[8,2,2048]{2,1,0:T(2,128)(2,1)S(1)} %all-to-all-done.4), channel_id=1, source_target_pairs={{0,256},{128,384},{256,0},{384,128},{1,257},{129,385},{257,1},{385... | collective-permute-start | bytes 196616 | tf_op jit(solution)/shard_map/ppermute | solution.py:18
  62.4 16.4 %all-to-all-done.2 = bf16[8,2,16,2048]{3,2,1,0:T(8,128)(2,1)} async-done(((bf16[8,2,16,2048]{3,2,1,0:T(8,128)(2,1)}), bf16[8,2,16,2048]{3,2,1,0:T(8,128)(2,1)}, u32[]{:S(2)}, u32[]{:S(2)}) %all-to-all-start.2) | async-done | bytes 1048608 | tf_op jit(solution)/shard_map/all_to_all | solution.py:78
  78.8 3.6 %all-to-all-start.3 = ((bf16[1,16,8,2,1024]{4,3,2,0,1:T(2,128)(2,1)}), bf16[1,16,8,2,1024]{4,3,2,0,1:T(2,128)(2,1)S(1)}, u32[]{:S(2)}, u32[]{:S(2)}) async-start(bf16[1,16,8,2,1024]{4,3,2,0,1:T(2,128)(2,1)} %bitcast.77), calls=%async_computation.3 | async-start | bytes 1048576 | tf_op jit(solution)/shard_map/all_to_all | solution.py:83
  82.4 2.9 %collective-permute-start = (bf16[8,2,16,2048]{3,2,1,0:T(8,128)(2,1)}, bf16[8,2,16,2048]{3,2,1,0:T(8,128)(2,1)S(1)}, u32[]{:S(2)}, u32[]{:S(2)}) collective-permute-start(bf16[8,2,16,2048]{3,2,1,0:T(8,128)(2,1)} %all-to-all-done.2), channel_id=1, source_target_pairs={{0,256},{128,384},{256,0},{384,128},{1,257},{129,385},{257,1},{385... | collective-permute-start | bytes 3145736 | tf_op jit(solution)/shard_map/ppermute | solution.py:18
  86.1 0.7 copy.51
  86.9 9.2 %all-to-all-done.3 = bf16[1,16,8,2,1024]{4,3,2,0,1:T(2,128)(2,1)S(1)} async-done(((bf16[1,16,8,2,1024]{4,3,2,0,1:T(2,128)(2,1)}), bf16[1,16,8,2,1024]{4,3,2,0,1:T(2,128)(2,1)S(1)}, u32[]{:S(2)}, u32[]{:S(2)}) %all-to-all-start.3) | async-done | bytes 524320 | tf_op jit(solution)/shard_map/all_to_all | solution.py:83
  96.1 5.0 %all-to-all-start.1 = ((bf16[2,16,1024]{2,0,1:T(2,128)(2,1)}), bf16[2,16,1024]{2,0,1:T(2,128)(2,1)S(1)}, u32[]{:S(2)}, u32[]{:S(2)}) async-start(bf16[2,16,1024]{2,0,1:T(2,128)(2,1)} %copy.51), calls=%async_computation.1 | async-start | bytes 131072 | tf_op jit(solution)/shard_map/all_to_all | solution.py:88
  102.1 14.2 %collective-permute-done = bf16[8,2,16,2048]{3,2,1,0:T(8,128)(2,1)S(1)} collective-permute-done((bf16[8,2,16,2048]{3,2,1,0:T(8,128)(2,1)}, bf16[8,2,16,2048]{3,2,1,0:T(8,128)(2,1)S(1)}, u32[]{:S(2)}, u32[]{:S(2)}) %collective-permute-start) | collective-permute-done | bytes 1048608 | tf_op jit(solution)/shard_map/ppermute | solution.py:18
  117.2 1.0 fusion.2
  118.3 12.9 %copy.59 = bf16[1,8,2,16384]{1,2,0,3:T(2,128)(2,1)} copy(bf16[1,8,2,16384]{3,2,1,0:T(2,128)(2,1)S(1)} %convert_element_type.88) | data formatting | bytes 1048576 | tf_op jit(solution)/shard_map/convert_element_type | solution.py:46
  131.3 9.1 %fusion.33 = bf16[16384,1,2,8]{3,2,1,0:T(2,128)(2,1)} fusion(bf16[1,8,2,16384]{1,2,0,3:T(2,128)(2,1)} %copy.59, bf16[8,2]{0,1:T(2,128)(2,1)S(1)} %collective-permute-done.2), kind=kLoop, calls=%fused_computation.54 | loop fusion | flops 262144 | bytes 1048608
  140.4 11.2 %reshape.155 = bf16[16,2,8192]{2,1,0:T(2,128)(2,1)} reshape(bf16[16384,1,2,8]{3,2,1,0:T(2,128)(2,1)} %fusion.33) | data formatting | bytes 1048576
  151.6 8.5 %all-to-all-start.6 = ((bf16[16,2,8192]{2,1,0:T(2,128)(2,1)}), bf16[16,2,8192]{2,1,0:T(2,128)(2,1)S(1)}, u32[]{:S(2)}, u32[]{:S(2)}) async-start(bf16[16,2,8192]{2,1,0:T(2,128)(2,1)} %reshape.155), calls=%async_computation.6 | async-start | bytes 1048576 | tf_op jit(solution)/shard_map/all_to_all | solution.py:96
  160.7 13.7 %all-to-all-done.6 = bf16[16,2,8192]{2,1,0:T(2,128)(2,1)S(1)} async-done(((bf16[16,2,8192]{2,1,0:T(2,128)(2,1)}), bf16[16,2,8192]{2,1,0:T(2,128)(2,1)S(1)}, u32[]{:S(2)}, u32[]{:S(2)}) %all-to-all-start.6) | async-done | bytes 524320 | tf_op jit(solution)/shard_map/all_to_all | solution.py:96
  174.4 10.9 %reshape.156 = bf16[16384,1,2,8]{3,2,1,0:T(2,128)(2,1)} reshape(bf16[16,2,8192]{2,1,0:T(2,128)(2,1)S(1)} %all-to-all-done.6) | data formatting | bytes 1048576
  185.3 11.6 %copy.69 = bf16[1,8,2,16,1024]{4,3,1,2,0:T(8,128)(2,1)S(1)} copy(bf16[1,8,2,16,1024]{1,2,4,3,0:T(2,128)(2,1)} %bitcast.67) | data formatting | bytes 1048576 | tf_op jit(solution)/shard_map/all_to_all | solution.py:96
  196.9 1.3 copy.61
  198.3 1.0 copy.91
  (46 shorter events, 7.4 us)
Async XLA Ops:
  0.6 9.9 %copy-start = (bf16[8,2048]{1,0:T(8,128)(2,1)S(1)}, bf16[8,2048]{1,0:T(8,128)(2,1)}, u32[]{:S(2)}) copy-start(bf16[8,2048]{1,0:T(8,128)(2,1)} %param.14) | copy-start | bytes 98308
  0.6 55.2 %copy-start.1 = (bf16[2,2048]{1,0:T(2,128)(2,1)S(1)}, bf16[2,2048]{1,0:T(2,128)(2,1)}, u32[]{:S(2)}) copy-start(bf16[2,2048]{1,0:T(2,128)(2,1)} %param.10) | copy-start | bytes 24580
  0.7 55.8 %copy-start.2 = (s32[2]{0:T(128)S(1)}, s32[2]{0:T(128)}, u32[]{:S(2)}) copy-start(s32[2]{0:T(128)} %param.11) | copy-start | bytes 28
  2.9 14.1 %all-to-all-start.5 = ((bf16[8,1,2]{2,1,0:T(2,128)(2,1)}), bf16[8,1,2]{2,1,0:T(2,128)(2,1)S(1)}, u32[]{:S(2)}, u32[]{:S(2)}) async-start(bf16[8,1,2]{2,1,0:T(2,128)(2,1)} %all_to_all.77), calls=%async_computation.5 | async-start | bytes 8192 | tf_op jit(solution)/shard_map/all_to_all | solution.py:80
  17.0 10.5 %all-to-all-start.4 = ((bf16[8,2,2048]{2,1,0:T(2,128)(2,1)}), bf16[8,2,2048]{2,1,0:T(2,128)(2,1)S(1)}, u32[]{:S(2)}, u32[]{:S(2)}) async-start(bf16[8,2,2048]{2,1,0:T(2,128)(2,1)} %reshape.140), calls=%async_computation.4 | async-start | bytes 131072 | tf_op jit(solution)/shard_map/all_to_all | solution.py:79
  27.5 21.8 %all-to-all-start = ((bf16[16,2,1024]{2,1,0:T(2,128)(2,1)}), bf16[16,2,1024]{2,1,0:T(2,128)(2,1)S(1)}, u32[]{:S(2)}, u32[]{:S(2)}) async-start(bf16[16,2,1024]{2,1,0:T(2,128)(2,1)} %all_to_all.60), calls=%async_computation | async-start | bytes 131072 | tf_op jit(solution)/shard_map/all_to_all | solution.py:84
  49.3 29.5 %all-to-all-start.2 = ((bf16[8,2,16,2048]{3,2,1,0:T(8,128)(2,1)}), bf16[8,2,16,2048]{3,2,1,0:T(8,128)(2,1)}, u32[]{:S(2)}, u32[]{:S(2)}) async-start(bf16[8,2,16,2048]{3,2,1,0:T(8,128)(2,1)} %bitcast.32), calls=%async_computation.2 | async-start | bytes 2097152 | tf_op jit(solution)/shard_map/all_to_all | solution.py:78
  56.6 74.7 %collective-permute-start.2 = (bf16[8,2]{0,1:T(2,128)(2,1)S(1)}, bf16[8,2]{0,1:T(2,128)(2,1)S(1)}, u32[]{:S(2)}, u32[]{:S(2)}) collective-permute-start(bf16[8,2]{0,1:T(2,128)(2,1)S(1)} %bitcast.86), channel_id=1, source_target_pairs={{0,256},{128,384},{256,0},{384,128},{1,257},{129,385},{257,1},{385... | collective-permute-start | bytes 104 | tf_op jit(solution)/shard_map/ppermute | solution.py:18
  59.5 27.3 %collective-permute-start.1 = (bf16[8,2,2048]{2,1,0:T(2,128)(2,1)S(1)}, bf16[8,2,2048]{2,1,0:T(2,128)(2,1)S(1)}, u32[]{:S(2)}, u32[]{:S(2)}) collective-permute-start(bf16[8,2,2048]{2,1,0:T(2,128)(2,1)S(1)} %all-to-all-done.4), channel_id=1, source_target_pairs={{0,256},{128,384},{256,0},{384,128},{1,257},{129,385},{257,1},{385... | collective-permute-start | bytes 196616 | tf_op jit(solution)/shard_map/ppermute | solution.py:18
  78.8 17.3 %all-to-all-start.3 = ((bf16[1,16,8,2,1024]{4,3,2,0,1:T(2,128)(2,1)}), bf16[1,16,8,2,1024]{4,3,2,0,1:T(2,128)(2,1)S(1)}, u32[]{:S(2)}, u32[]{:S(2)}) async-start(bf16[1,16,8,2,1024]{4,3,2,0,1:T(2,128)(2,1)} %bitcast.77), calls=%async_computation.3 | async-start | bytes 1048576 | tf_op jit(solution)/shard_map/all_to_all | solution.py:83
  82.4 33.8 %collective-permute-start = (bf16[8,2,16,2048]{3,2,1,0:T(8,128)(2,1)}, bf16[8,2,16,2048]{3,2,1,0:T(8,128)(2,1)S(1)}, u32[]{:S(2)}, u32[]{:S(2)}) collective-permute-start(bf16[8,2,16,2048]{3,2,1,0:T(8,128)(2,1)} %all-to-all-done.2), channel_id=1, source_target_pairs={{0,256},{128,384},{256,0},{384,128},{1,257},{129,385},{257,1},{385... | collective-permute-start | bytes 3145736 | tf_op jit(solution)/shard_map/ppermute | solution.py:18
  96.1 55.5 %all-to-all-start.1 = ((bf16[2,16,1024]{2,0,1:T(2,128)(2,1)}), bf16[2,16,1024]{2,0,1:T(2,128)(2,1)S(1)}, u32[]{:S(2)}, u32[]{:S(2)}) async-start(bf16[2,16,1024]{2,0,1:T(2,128)(2,1)} %copy.51), calls=%async_computation.1 | async-start | bytes 131072 | tf_op jit(solution)/shard_map/all_to_all | solution.py:88
  151.6 22.8 %all-to-all-start.6 = ((bf16[16,2,8192]{2,1,0:T(2,128)(2,1)}), bf16[16,2,8192]{2,1,0:T(2,128)(2,1)S(1)}, u32[]{:S(2)}, u32[]{:S(2)}) async-start(bf16[16,2,8192]{2,1,0:T(2,128)(2,1)} %reshape.155), calls=%async_computation.6 | async-start | bytes 1048576 | tf_op jit(solution)/shard_map/all_to_all | solution.py:96
where the time goes:
time: 203 us; the launch traced here: 199 us
  waiting for transfers between devices  70.4 us (35%)
  local copies, waits for them, and re-layouts  59.8 us (29%)
  starting transfers between devices  53.1 us (26%)
  other arithmetic  11.4 us (6%)
  matrix products  3.51 us (2%)
    unnamed x17, local copies, waits for them, and re-layouts  28.5 us
    all_to_all x1, waiting for transfers between devices, body(): lax.all_to_all(outgoing[0], 'grp', split_axis=0, concat_axis=0, tiled=True)  16.4 us
    ppermute x3, waiting for transfers between devices, from_behind(): lax.ppermute(array, axis, [(i, (i + by) % devices) for i in range(devices)])  14.2 us
    convert_element_type x4, local copies, waits for them, and re-layouts, attend(): (numer / totals[..., None]).reshape(count, QH * HD).astype(jnp.bfloat16)  13.8 us
    all_to_all x1, waiting for transfers between devices, body(): lax.all_to_all(hand_out, 'tp', split_axis=3, concat_axis=0, tiled=True)  13.7 us
    all_to_all x1, starting transfers between devices, body(): lax.all_to_all(resident_query, 'tp', split_axis=0, concat_axis=1, tiled=T...  12.6 us
    all_to_all x1, local copies, waits for them, and re-layouts, body(): lax.all_to_all(hand_out, 'tp', split_axis=3, concat_axis=0, tiled=True)  11.6 us
    all_to_all x1, waiting for transfers between devices, body(): lax.all_to_all(handed_query, 'tp', split_axis=1, concat_axis=4, tiled=True)  9.24 us
  transfers between devices with their start and end apart: 10, of which 7 were waited for; matrix products, arithmetic and copies ran while one was open for 23% of the time, Pallas kernels for 0%

commit v1 on v0

v1 whole, which is shorter than its diff:
```python
import functools
import math

import jax
import jax.numpy as jnp
from jax import lax
from jax.experimental import pallas as pl
from jax.experimental.pallas import tpu as pltpu
from jax.sharding import PartitionSpec as P

MESH = pl.DeviceIdType.MESH
BF = jnp.bfloat16
F32 = jnp.float32
HD = 128
KVH = 8
N_GRP = 8
N_TP = 16
NEG_FILL = -1e30
SCALE = 1.0 / math.sqrt(HD)
HC = 2
NCH = KVH // HC
W = HC * HD


def iota(shape, dim):
    return lax.broadcasted_iota(jnp.int32, shape, dim)


def attend(q, k, v, new_k, new_v, valid):
    s = lax.dot_general(q, k, (((1,), (1,)), ((), ())), preferred_element_type=F32) * SCALE
    s = jnp.where(valid, s, NEG_FILL)
    sn = jnp.sum(q.astype(F32) * new_k, axis=-1, keepdims=True) * SCALE
    top = jnp.maximum(jnp.max(s, axis=-1, keepdims=True), sn)
    p = jnp.exp(s - top)
    pn = jnp.exp(sn - top)
    total = jnp.sum(p, axis=-1, keepdims=True) + pn
    numer = jnp.dot(p.astype(BF), v, preferred_element_type=F32)
    numer = numer + pn.astype(BF).astype(F32) * new_v
    return (numer / total).astype(BF)


def kernel(
    kv_any, rq_ref, rn_ref, len_ref, fkv_any, hq_any, fn_ref, mt_ref,
    ro_ref, ho_any, hc_any,
    rkv, rqf, rqt, rqs, rqb, ros, rob, rof, rot, place_s, place_r, new_s, new_r,
    npk, nb, land, sel, pk, kvb, qb, osd,
    loc, cps, pls, plr, nws, nwr, s1s, s1r, nys, nyr, s2s, s2r, rqss, rqr, qs, qr, rosm, ror, os_, orr,
):
    side = lax.axis_index("side")
    g = lax.axis_index("grp")
    i = lax.axis_index("tp")
    sp = (side + 2) % 4
    c0 = i // (2 * HC)

    def remote(src, dst, ss, rs, **dev):
        return pltpu.make_async_remote_copy(
            src_ref=src, dst_ref=dst, send_sem=ss, recv_sem=rs, device_id=dev, device_id_type=MESH
        )

    def over(n, f):
        def body(k, _):
            f(k)
            return 0

        lax.fori_loop(0, n, body, 0)

    def d_stage1(c, part):
        cols = pl.ds(pl.multiple_of(part * KVH * HD + c * W, 128), W)
        return remote(
            fkv_any.at[:, :, cols], land.at[c, :, :, pl.ds(part * W, W)],
            s1s.at[c, part], s1r.at[c, part], side=sp,
        )

    def d_place():
        return remote(place_s, place_r, pls, plr, side=sp)

    def d_new():
        return remote(new_s, new_r, nws, nwr, side=sp)

    def d_new_y(d, me):
        return remote(npk.at[d], nb.at[me], nys.at[d], nyr.at[me], grp=d)

    def d_kv_y(c, d, me):
        return remote(pk.at[c, d], kvb.at[c, me], s2s.at[c, d], s2r.at[c, me], grp=d)

    def d_rq(t, me):
        return remote(rqs.at[t], rqb.at[me], rqss.at[t], rqr.at[me], tp=t)

    def d_q(t, me):
        return remote(hq_any.at[t], qb.at[me], qs.at[t], qr.at[me], tp=t)

    def d_ro(t, me):
        return remote(ros.at[t], rob.at[me], rosm.at[t], ror.at[me], tp=t)

    def d_out(t, me):
        return remote(osd.at[t], ho_any.at[me], os_.at[t], orr.at[me], tp=t)

    def l_kv():
        return pltpu.make_async_copy(kv_any, rkv, loc.at[0])

    def l_q():
        return pltpu.make_async_copy(hq_any.at[i], qb.at[i], loc.at[1])

    def l_out():
        return pltpu.make_async_copy(osd.at[i], ho_any.at[i], loc.at[2])

    def l_cache(c, part):
        cols = pl.ds(pl.multiple_of(part * KVH * HD + c * W, 128), W)
        return pltpu.make_async_copy(
            kvb.at[c, :, :, pl.ds(part * W, W)], hc_any.at[:, :, cols], cps.at[c, part]
        )

    def tp_peer(k):
        return (i + N_TP - 1 - k) % N_TP

    def grp_peer(k):
        return (g + 1 + k) % N_GRP

    l_kv().start()
    l_q().start()
    barrier = pltpu.get_barrier_semaphore()
    pl.semaphore_signal(barrier, inc=1, device_id={"side": sp}, device_id_type=MESH)
    over(N_GRP - 1, lambda k: pl.semaphore_signal(
        barrier, inc=1, device_id={"grp": grp_peer(k)}, device_id_type=MESH))
    over(N_TP - 1, lambda k: pl.semaphore_signal(
        barrier, inc=1, device_id={"tp": tp_peer(k)}, device_id_type=MESH))

    m = jnp.broadcast_to(mt_ref[...], (8, 128))
    row, lane = iota((8, 128), 0), iota((8, 128), 1)

    def places(req):
        mrow = jnp.sum(jnp.where(row == req, m, 0), axis=0, keepdims=True)
        mine = jnp.broadcast_to(mrow, (8, 128))
        rank = jnp.sum(jnp.where((m == mine) & (row < req), 1, 0), axis=0, keepdims=True)
        return jnp.broadcast_to(mrow * 2 + rank, (8, 128))

    wide = places(lane // 16) * 16 + lane % 16
    narrow = jnp.where(lane < 8, places(lane), -1)
    place_s[...] = jnp.where(row < 4, wide, narrow)
    new_s[...] = jnp.concatenate([fn_ref[...], jnp.zeros((8, 2 * KVH * HD), BF)], axis=0)
    for j in range(8):
        rqf[32 * j:32 * j + 32] = rq_ref[:, 128 * j:128 * j + 128].astype(F32)
    for j in range(8):
        for r in range(2):
            rqt[pl.ds(2 * j + r, 16, stride=16), :] = rqf[pl.ds(32 * j + r, 16, stride=2), :]
    rqs[...] = rqt[...].astype(BF).reshape(16, 16, 128)
    rqb[i] = rqs[i]

    pl.semaphore_wait(barrier, N_TP + N_GRP - 1)

    d_place().start()

    def start1(t):
        c = (c0 + t) % NCH
        d_stage1(c, 0).start()
        d_stage1(c, 1).start()

    over(NCH, start1)
    d_new().start()
    over(N_TP - 1, lambda k: d_rq(tp_peer(k), i).start())
    over(N_TP - 1, lambda k: d_q(tp_peer(k), i).start())

    d_place().wait_recv()
    sel[...] = jnp.where(iota((256, 128), 0) == place_r[0:1, :], 1.0, 0.0).astype(BF)
    sel16 = jnp.where(iota((16, 16), 0) == place_r[4:5, 0:16], 1.0, 0.0).astype(BF)

    def pack(t):
        c = (c0 + t) % NCH
        d_stage1(c, 0).wait_recv()
        d_stage1(c, 1).wait_recv()
        x = land[c].reshape(128, 2 * W)
        y = jnp.dot(sel[...], x, preferred_element_type=F32).astype(BF)
        pk[c] = y.reshape(8, 32, 2 * W)
        over(N_GRP - 1, lambda k: d_kv_y(c, grp_peer(k), g).start())
        kvb[c, g] = pk[c, g]

    over(NCH, pack)

    d_new().wait_recv()
    for c in range(16):
        cols = slice(128 * c, 128 * c + 128)
        y = jnp.dot(sel16, new_r[:, cols], preferred_element_type=F32).astype(BF)
        npk[:, :, cols] = y.reshape(8, 2, 128)
    over(N_GRP - 1, lambda k: d_new_y(grp_peer(k), g).start())
    nb[g] = npk[g]

    l_kv().wait()
    over(N_TP - 1, lambda k: d_rq(tp_peer(k), tp_peer(k)).wait_recv())
    rrow, rcol = iota((32, 512), 0) % 2, iota((32, 512), 1)
    length = jnp.where(rrow == 0, len_ref[0], len_ref[1])
    rvalid = (rcol // 256 == rrow) & (rcol % 256 < length)
    first = iota((32, 128), 0) % 2 == 0

    def resident(h):
        q = jnp.concatenate([rqb[2 * h], rqb[2 * h + 1]], axis=0)
        kcols = pl.ds(pl.multiple_of(h * 128, 128), 128)
        vcols = pl.ds(pl.multiple_of(KVH * HD + h * 128, 128), 128)
        k = rkv[:, :, kcols].reshape(512, 128)
        v = rkv[:, :, vcols].reshape(512, 128)
        nk = rn_ref[:, kcols].astype(F32)
        nv = rn_ref[:, vcols].astype(F32)
        o = attend(
            q, k, v, jnp.where(first, nk[0:1], nk[1:2]), jnp.where(first, nv[0:1], nv[1:2]), rvalid
        )
        ros[2 * h] = o[0:16]
        ros[2 * h + 1] = o[16:32]

    over(KVH, resident)
    over(N_TP - 1, lambda k: d_ro(tp_peer(k), i).start())
    rob[i] = ros[i]

    over(N_GRP - 1, lambda k: d_new_y(grp_peer(k), grp_peer(k)).wait_recv())
    l_q().wait()
    hvalid = iota((256, 256), 0) % 16 == iota((256, 256), 1) // 16

    def handed(t):
        c = (c0 + t) % NCH
        over(N_GRP - 1, lambda k: d_kv_y(c, grp_peer(k), grp_peer(k)).wait_recv())
        l_cache(c, 0).start()
        l_cache(c, 1).start()
        for u in range(HC):
            h = c * HC + u
            for t2 in range(2):
                @pl.when(2 * h + t2 != i)
                def _():
                    d_q(2 * h + t2, 2 * h + t2).wait_recv()
            q = jnp.concatenate(
                [
                    qb[2 * h + t2, :, :, 128 * j:128 * j + 128].reshape(16, 128)
                    for t2 in range(2) for j in range(8)
                ],
                axis=0,
            )
            k = kvb[c, :, :, 128 * u:128 * u + 128].reshape(256, 128)
            v = kvb[c, :, :, W + 128 * u:W + 128 * u + 128].reshape(256, 128)
            kcols = pl.ds(pl.multiple_of(h * 128, 128), 128)
            vcols = pl.ds(pl.multiple_of(KVH * HD + h * 128, 128), 128)
            nk = nb[:, :, kcols].reshape(16, 128).astype(F32)
            nv = nb[:, :, vcols].reshape(16, 128).astype(F32)
            o = attend(q, k, v, jnp.tile(nk, (16, 1)), jnp.tile(nv, (16, 1)), hvalid)
            for t2 in range(2):
                for j in range(8):
                    at = 16 * (8 * t2 + j)
                    osd[2 * h + t2, :, :, 128 * j:128 * j + 128] = o[at:at + 16].reshape(8, 2, 128)
            for t2 in range(2):
                @pl.when(2 * h + t2 != i)
                def _():
                    d_out(2 * h + t2, i).start()

    over(NCH, handed)
    l_out().start()

    over(N_TP - 1, lambda k: d_ro(tp_peer(k), tp_peer(k)).wait_recv())
    rof[...] = rob[...].reshape(256, 128).astype(F32)
    for j in range(8):
        for r in range(2):
            rot[pl.ds(32 * j + r, 16, stride=2), :] = rof[pl.ds(2 * j + r, 16, stride=16), :]
    for j in range(8):
        ro_ref[:, 128 * j:128 * j + 128] = rot[32 * j:32 * j + 32].astype(BF)

    d_place().wait_send()
    d_new().wait_send()

    def end_chunk(c):
        for part in range(2):
            d_stage1(c, part).wait_send()
            l_cache(c, part).wait()
        over(N_GRP - 1, lambda k: d_kv_y(c, grp_peer(k), g).wait_send())

    over(NCH, end_chunk)
    over(N_GRP - 1, lambda k: d_new_y(grp_peer(k), g).wait_send())

    def end_tp(k):
        t = tp_peer(k)
        d_rq(t, i).wait_send()
        d_q(t, i).wait_send()
        d_ro(t, i).wait_send()
        d_out(t, i).wait_send()
        d_out(t, t).wait_recv()

    over(N_TP - 1, end_tp)
    l_out().wait()


def body(
    resident_kv, resident_query, resident_new, lengths, fresh_kv, handed_query, fresh_new, matching
):
    vm = pl.BlockSpec(memory_space=pltpu.VMEM)
    sm = pl.BlockSpec(memory_space=pltpu.SMEM)
    anys = pl.BlockSpec(memory_space=pl.ANY)
    dma = pltpu.SemaphoreType.DMA
    ro, ho, hc = pl.pallas_call(
        kernel,
        out_shape=(
            jax.ShapeDtypeStruct((32, 1024), BF),
            jax.ShapeDtypeStruct((16, 8, 2, 1024), BF),
            jax.ShapeDtypeStruct((8, 32, 2048), BF),
        ),
        in_specs=[anys, vm, vm, sm, anys, anys, vm, vm],
        out_specs=(vm, anys, anys),
        scratch_shapes=[
            pltpu.VMEM((2, 256, 2048), BF),
            pltpu.VMEM((256, 128), F32),
            pltpu.VMEM((256, 128), F32),
            pltpu.VMEM((16, 16, 128), BF),
            pltpu.VMEM((16, 16, 128), BF),
            pltpu.VMEM((16, 16, 128), BF),
            pltpu.VMEM((16, 16, 128), BF),
            pltpu.VMEM((256, 128), F32),
            pltpu.VMEM((256, 128), F32),
            pltpu.VMEM((8, 128), jnp.int32),
            pltpu.VMEM((8, 128), jnp.int32),
            pltpu.VMEM((16, 2048), BF),
            pltpu.VMEM((16, 2048), BF),
            pltpu.VMEM((8, 2, 2048), BF),
            pltpu.VMEM((8, 2, 2048), BF),
            pltpu.VMEM((NCH, 8, 16, 2 * W), BF),
            pltpu.VMEM((256, 128), BF),
            pltpu.VMEM((NCH, 8, 32, 2 * W), BF),
            pltpu.VMEM((NCH, 8, 32, 2 * W), BF),
            pltpu.VMEM((16, 8, 2, 1024), BF),
            pltpu.VMEM((16, 8, 2, 1024), BF),
            dma((3,)), dma((NCH, 2)),
            dma, dma, dma, dma,
            dma((NCH, 2)), dma((NCH, 2)),
            dma((8,)), dma((8,)),
            dma((NCH, 8)), dma((NCH, 8)),
            dma((16,)), dma((16,)), dma((16,)), dma((16,)),
            dma((16,)), dma((16,)), dma((16,)), dma((16,)),
        ],
        compiler_params=pltpu.CompilerParams(
            collective_id=0, has_side_effects=True, vmem_limit_bytes=48 * 1024 * 1024
        ),
        name="handoff",
    )(
        resident_kv, resident_query, resident_new, lengths, fresh_kv,
        handed_query.reshape(16, 8, 2, 1024), fresh_new, matching,
    )
    return (
        ro,
        ho.reshape(1, 16, 8, 2, 1024),
        hc.reshape(1, 1, 8, 2, 16, 2048),
    )


def solution(mesh):
    return jax.shard_map(
        body,
        mesh=mesh,
        in_specs=(
            P(("side", "grp", "tp"), None, None),
            P(("side", "grp"), "tp"),
            P(("side", "grp", "tp"), None),
            P(("side", "grp", "tp")),
            P(("side", "grp", "tp"), None, None),
            P(("side", "grp"), None, None, None, "tp"),
            P(("side", "grp", "tp"), None),
            P(("side", "grp", "tp"), None),
        ),
        out_specs=(
            P(("side", "grp"), "tp"),
            P(("side", "grp"), None, None, None, "tp"),
            P(("side", "grp"), "tp", None, None, None, None),
        ),
        check_vma=False,
    )
```

time: 203 us -> 77.4 us (0.38); the launches traced: 199 us -> 77 us
  waiting for transfers between devices: 70.4 us -> 0 us
  Pallas kernels: 0 us -> 66.6 us
  starting transfers between devices: 53.1 us -> 0 us
  local copies, waits for them, and re-layouts: 59.8 us -> 9.74 us
  other arithmetic: 11.4 us -> 0 us
  matrix products: 3.51 us -> 0 us
    pallas_call x0 -> x1, Pallas kernels: none -> 66.6 us  [body(): pl.pallas_call(kernel, out_shape=(jax.ShapeDtypeStruct((32, 1024), BF), j...]
    all_to_all x7 -> x0, waiting for transfers between devices: 56.2 us -> none  [the longest x1 16.4 us: body(): lax.all_to_all(outgoing[0], 'grp', split_axis=0, concat_axis=0, tiled=True)]
    all_to_all x7 -> x0, starting transfers between devices: 44.9 us -> none  [the longest x1 12.6 us: body(): lax.all_to_all(resident_query, 'tp', split_axis=0, concat_axis=1, tiled=T...]
    unnamed x17 -> x18, local copies, waits for them, and re-layouts: 28.5 us -> 9.74 us
    all_to_all x7 -> x0, local copies, waits for them, and re-layouts: 14.8 us -> none  [the longest x1 11.6 us: body(): lax.all_to_all(hand_out, 'tp', split_axis=3, concat_axis=0, tiled=True)]
    ppermute x3 -> x0, waiting for transfers between devices: 14.2 us -> none  [from_behind(): lax.ppermute(array, axis, [(i, (i + by) % devices) for i in range(devices)])]
    convert_element_type x4 -> x0, local copies, waits for them, and re-layouts: 13.8 us -> none  [attend(): (numer / totals[..., None]).reshape(count, QH * HD).astype(jnp.bfloat16)]
    unnamed x3 -> x0, other arithmetic: 9.16 us -> none
  transfers between devices with their start and end apart: 10 -> 0, of which waited for: 7 -> 0; matrix products, arithmetic and copies ran while one was open for 23% -> 0% of each run, Pallas kernels for 0% -> 0%
where the time goes in v1:
time: 77.4 us; the launch traced here: 77 us
  Pallas kernels  66.6 us (86%)
  local copies, waits for them, and re-layouts  9.74 us (13%)
    pallas_call x1, Pallas kernels, body(): pl.pallas_call(kernel, out_shape=(jax.ShapeDtypeStruct((32, 1024), BF), j...  66.6 us
    unnamed x18, local copies, waits for them, and re-layouts  9.74 us

profile of v1, /device:TPU:1, one launch (start us, length us, event | category | flops | bytes accessed | tf_op | source)
XLA Modules:
  0.0 77.0 jit_solution(9058716658742931949)
XLA Ops:
  0.6 0.7 copy.11.mt_ref
  1.4 0.0 copy-start
  1.4 1.6 %copy-done = bf16[2,256,2048]{2,1,0:T(8,128)(2,1)S(1)} copy-done((bf16[2,256,2048]{2,1,0:T(8,128)(2,1)S(1)}, bf16[2,256,2048]{2,1,0:T(8,128)(2,1)}, u32[]{:S(2)}) %copy-start) | copy-done | bytes 2097176
  3.0 0.0 copy-start.1
  3.0 1.0 %copy-done.1 = bf16[8,16,2048]{2,1,0:T(8,128)(2,1)S(1)} copy-done((bf16[8,16,2048]{2,1,0:T(8,128)(2,1)S(1)}, bf16[8,16,2048]{2,1,0:T(8,128)(2,1)}, u32[]{:S(2)}) %copy-start.1) | copy-done | bytes 524312
  4.0 0.0 copy-start.2
  4.0 1.0 %copy-done.2 = bf16[1,16,8,2,1024]{4,3,2,1,0:T(2,128)(2,1)S(1)} copy-done((bf16[1,16,8,2,1024]{4,3,2,1,0:T(2,128)(2,1)S(1)}, bf16[1,16,8,2,1024]{4,3,2,1,0:T(2,128)(2,1)}, u32[]{:S(2)}) %copy-start.2) | copy-done | bytes 524312
  5.0 0.0 copy-start.3
  5.0 0.8 %copy-done.3 = bf16[32,1024]{1,0:T(8,128)(2,1)S(1)} copy-done((bf16[32,1024]{1,0:T(8,128)(2,1)S(1)}, bf16[32,1024]{1,0:T(8,128)(2,1)}, u32[]{:S(2)}) %copy-start.3) | copy-done | bytes 65560
  5.9 0.0 copy-start.4
  5.9 0.8 copy-done.4
  6.6 0.0 copy-start.5
  6.6 0.7 copy-done.5
  7.3 0.0 copy-start.6
  7.3 0.7 copy-done.6
  8.0 66.6 %handoff.1 = (bf16[32,1024]{1,0:T(8,128)(2,1)S(1)}, bf16[16,8,2,1024]{3,2,1,0:T(2,128)(2,1)S(1)}, bf16[8,32,2048]{2,1,0:T(8,128)(2,1)S(1)}) custom-call(bf16[2,256,2048]{2,1,0:T(8,128)(2,1)S(1)} %copy-done, bf16[32,1024]{1,0:T(8,128)(2,1)S(1)} %copy-done.3, bf16[2,2048]{1,0:T(2,128)(2,1)S(1)} %copy-done.5, s32[2]{0:T(128)S(1)} %copy-done.6, ...), custom_call_target="tpu_custom_call" | custom-call | tf_op jit(solution)/shard_map/handoff/pallas_call | solution.py:292
  74.6 0.6 copy.15
  75.3 0.8 %copy.16 = bf16[1,16,8,2,1024]{4,3,2,1,0:T(2,128)(2,1)} copy(bf16[1,16,8,2,1024]{4,3,2,1,0:T(2,128)(2,1)S(1)} %bitcast.4) | data formatting | bytes 1048576
  76.1 1.0 %copy.17 = bf16[1,1,8,2,16,2048]{5,4,3,2,1,0:T(8,128)(2,1)} copy(bf16[1,1,8,2,16,2048]{5,4,3,2,1,0:T(8,128)(2,1)S(1)} %bitcast.3) | data formatting | bytes 2097152
Async XLA Ops:
  1.4 1.6 %copy-start = (bf16[2,256,2048]{2,1,0:T(8,128)(2,1)S(1)}, bf16[2,256,2048]{2,1,0:T(8,128)(2,1)}, u32[]{:S(2)}) copy-start(bf16[2,256,2048]{2,1,0:T(8,128)(2,1)} %kv_any.1) | copy-start | bytes 6291460
  3.0 1.0 %copy-start.1 = (bf16[8,16,2048]{2,1,0:T(8,128)(2,1)S(1)}, bf16[8,16,2048]{2,1,0:T(8,128)(2,1)}, u32[]{:S(2)}) copy-start(bf16[8,16,2048]{2,1,0:T(8,128)(2,1)} %fkv_any.1) | copy-start | bytes 1572868
  4.0 1.0 %copy-start.2 = (bf16[1,16,8,2,1024]{4,3,2,1,0:T(2,128)(2,1)S(1)}, bf16[1,16,8,2,1024]{4,3,2,1,0:T(2,128)(2,1)}, u32[]{:S(2)}) copy-start(bf16[1,16,8,2,1024]{4,3,2,1,0:T(2,128)(2,1)} %param.13) | copy-start | bytes 1572868
  5.0 0.8 %copy-start.3 = (bf16[32,1024]{1,0:T(8,128)(2,1)S(1)}, bf16[32,1024]{1,0:T(8,128)(2,1)}, u32[]{:S(2)}) copy-start(bf16[32,1024]{1,0:T(8,128)(2,1)} %rq_ref.1) | copy-start | bytes 196612
  5.9 0.8 copy-start.4
  6.6 0.7 copy-start.5
  7.3 0.7 copy-start.6

commit v2 on v1

v2 whole, which is shorter than its diff:
```python
import math

import jax
import jax.numpy as jnp
from jax import lax
from jax.experimental import pallas as pl
from jax.experimental.pallas import tpu as pltpu
from jax.sharding import PartitionSpec as P

MESH = pl.DeviceIdType.MESH
BF = jnp.bfloat16
F32 = jnp.float32
HD = 128
KVH = 8
N_GRP = 8
N_TP = 16
NEG_FILL = -1e30
SCALE = 1.0 / math.sqrt(HD)
LAG = 2
FIRST = "kkqkqkqkqkkk"
LAST = "kkkkkqkqkqkq"


def iota(shape, dim):
    return lax.broadcasted_iota(jnp.int32, shape, dim)


def attend(q, k, v, new_k, new_v, valid):
    s = lax.dot_general(q, k, (((1,), (1,)), ((), ())), preferred_element_type=F32) * SCALE
    s = jnp.where(valid, s, NEG_FILL)
    sn = jnp.sum(q.astype(F32) * new_k, axis=-1, keepdims=True) * SCALE
    top = jnp.maximum(jnp.max(s, axis=-1, keepdims=True), sn)
    p = jnp.exp(s - top)
    pn = jnp.exp(sn - top)
    total = jnp.sum(p, axis=-1, keepdims=True) + pn
    numer = jnp.dot(p.astype(BF), v, preferred_element_type=F32)
    numer = numer + pn.astype(BF).astype(F32) * new_v
    return (numer / total).astype(BF)


def kernel(
    kv_any, rq_any, rn_any, len_any, fkv_any, hq_any, fn_any, mt_any,
    ro_ref, ho_ref, kvb,
    rq_v, rn_v, len_s, fn_v, mt_v,
    rkv, rqf, rqt, rqs, rqb, ros, rob, rof, rot, place_s, place_r, new_s, new_r,
    npk, nb, land, sel, pk, qb, osd,
    loc, pls, plr, nws, nwr, s1s, s1r, nys, nyr, s2s, s2r, rqss, rqr, qs, qr, rosm, ror, os_, orr,
):
    side = lax.axis_index("side")
    g = lax.axis_index("grp")
    i = lax.axis_index("tp")
    sp = (side + 2) % 4
    x, zh = i // 4, i % 4

    def head(p):
        return 2 * ((x + p) % 4) + p // 4

    def remote(src, dst, ss, rs, **dev):
        return pltpu.make_async_remote_copy(
            src_ref=src, dst_ref=dst, send_sem=ss, recv_sem=rs, device_id=dev, device_id_type=MESH
        )

    def span(low, high, f):
        def body(k, _):
            f(k)
            return 0

        lax.fori_loop(low, high, body, 0)

    def over(n, f):
        def body(k, _):
            f(k)
            return 0

        lax.fori_loop(0, n, body, 0)

    def d_stage1(h, part):
        cols = pl.ds(pl.multiple_of(part * KVH * HD + h * HD, 128), HD)
        return remote(
            fkv_any.at[:, :, cols], land.at[h, :, :, pl.ds(part * HD, HD)],
            s1s.at[h, part], s1r.at[h, part], side=sp,
        )

    def d_place():
        return remote(place_s, place_r, pls, plr, side=sp)

    def d_new():
        return remote(new_s, new_r, nws, nwr, side=sp)

    def d_new_y(d, me):
        return remote(npk.at[d], nb.at[me], nys.at[d], nyr.at[me], grp=d)

    def d_kv_y(c, d, me):
        return remote(pk.at[c, d], kvb.at[c, me], s2s.at[c, d], s2r.at[c, me], grp=d)

    def d_rq(t, me):
        return remote(rqs.at[t], rqb.at[me], rqss.at[t], rqr.at[me], tp=t)

    def d_q(t, me):
        return remote(hq_any.at[t], qb.at[me], qs.at[t], qr.at[me], tp=t)

    def d_ro(t, me):
        return remote(ros.at[t], rob.at[me], rosm.at[t], ror.at[me], tp=t)

    def d_out(t, me):
        return remote(osd.at[t], ho_ref.at[me], os_.at[t], orr.at[me], tp=t)

    def local(src, dst, at):
        return pltpu.make_async_copy(src, dst, loc.at[at])

    def l_kv():
        return local(kv_any, rkv, 0)

    def l_q():
        return local(hq_any.at[i], qb.at[i], 1)

    def l_out():
        return local(osd.at[i], ho_ref.at[i], 2)

    small = [
        local(mt_any, mt_v, 3), local(rq_any, rq_v, 4), local(fn_any, fn_v, 5),
        local(rn_any, rn_v, 6), local(len_any, len_s, 7),
    ]

    def tp_peer(k):
        return (i + N_TP - 1 - k) % N_TP

    def grp_peer(k):
        return (g + 1 + k) % N_GRP

    barrier = pltpu.get_barrier_semaphore()
    over(N_TP - 1, lambda k: pl.semaphore_signal(
        barrier, inc=1, device_id={"tp": tp_peer(k)}, device_id_type=MESH))
    over(N_GRP - 1, lambda k: pl.semaphore_signal(
        barrier, inc=1, device_id={"grp": grp_peer(k)}, device_id_type=MESH))
    pl.semaphore_signal(barrier, inc=1, device_id={"side": sp}, device_id_type=MESH)
    for copy in small:
        copy.start()
    l_q().start()
    l_kv().start()
    for copy in small:
        copy.wait()

    row, lane = iota((8, 128), 0), iota((8, 128), 1)
    across = jnp.broadcast_to(mt_v[...], (8, 8))
    down = jnp.sum(jnp.where(iota((8, 8), 0) == iota((8, 8), 1), across, 0), axis=1, keepdims=True)
    m = jnp.broadcast_to(down, (8, 128))

    def places(req):
        mrow = jnp.sum(jnp.where(row == req, m, 0), axis=0, keepdims=True)
        mine = jnp.broadcast_to(mrow, (8, 128))
        rank = jnp.sum(jnp.where((m == mine) & (row < req), 1, 0), axis=0, keepdims=True)
        return jnp.broadcast_to(mrow * 2 + rank, (8, 128))

    wide = places(lane // 16) * 16 + lane % 16
    narrow = jnp.where(lane < 8, places(lane), -1)
    place_s[...] = jnp.where(row < 4, wide, narrow)
    new_s[...] = jnp.concatenate([fn_v[...], jnp.zeros((8, 2 * KVH * HD), BF)], axis=0)
    for j in range(8):
        rqf[32 * j:32 * j + 32] = rq_v[:, 128 * j:128 * j + 128].astype(F32)
    for j in range(8):
        for r in range(2):
            rqt[pl.ds(2 * j + r, 16, stride=16), :] = rqf[pl.ds(32 * j + r, 16, stride=2), :]
    rqs[...] = rqt[...].astype(BF).reshape(16, 16, 128)
    rqb[i] = rqs[i]

    pl.semaphore_wait(barrier, N_TP + N_GRP - 1)

    def send_all(turns):
        k = q = 0
        for turn in turns:
            if turn == "k":
                d_stage1(head(k), 0).start()
                d_stage1(head(k), 1).start()
                k += 1
            else:
                for dz in range(4):
                    if q or dz:
                        d_q((x + 4 - q) % 4 * 4 + (zh + dz) % 4, i).start()
                q += 1
            if k == 1 and q == 0:
                over(N_TP - 1, lambda n: d_rq(tp_peer(n), i).start())

    d_place().start()
    d_new().start()

    @pl.when(zh < 2)
    def _():
        send_all(FIRST)

    @pl.when(zh >= 2)
    def _():
        send_all(LAST)

    d_place().wait_recv()
    sel[...] = jnp.where(iota((256, 128), 0) == place_r[0:1, :], 1.0, 0.0).astype(BF)
    sel16 = jnp.where(iota((16, 16), 0) == place_r[4:5, 0:16], 1.0, 0.0).astype(BF)

    def pack(p):
        h = head(p)
        d_stage1(h, 0).wait_recv()
        d_stage1(h, 1).wait_recv()
        x = land[h].reshape(128, 2 * HD)
        y = jnp.dot(sel[...], x, preferred_element_type=F32).astype(BF)
        pk[h] = y.reshape(8, 32, 2 * HD)
        over(N_GRP - 1, lambda k: d_kv_y(h, grp_peer(k), g).start())
        kvb[h, g] = pk[h, g]

    def pack_new():
        d_new().wait_recv()
        for c in range(16):
            cols = slice(128 * c, 128 * c + 128)
            y = jnp.dot(sel16, new_r[:, cols], preferred_element_type=F32).astype(BF)
            npk[:, :, cols] = y.reshape(8, 2, 128)
        over(N_GRP - 1, lambda k: d_new_y(grp_peer(k), g).start())
        nb[g] = npk[g]

    rrow, rcol = iota((32, 512), 0) % 2, iota((32, 512), 1)
    length = jnp.where(rrow == 0, len_s[0], len_s[1])
    rvalid = (rcol // 256 == rrow) & (rcol % 256 < length)
    first = iota((32, 128), 0) % 2 == 0

    def resident(h):
        q = jnp.concatenate([rqb[2 * h], rqb[2 * h + 1]], axis=0)
        kcols = pl.ds(pl.multiple_of(h * 128, 128), 128)
        vcols = pl.ds(pl.multiple_of(KVH * HD + h * 128, 128), 128)
        k = rkv[:, :, kcols].reshape(512, 128)
        v = rkv[:, :, vcols].reshape(512, 128)
        nk = rn_v[:, kcols].astype(F32)
        nv = rn_v[:, vcols].astype(F32)
        o = attend(
            q, k, v, jnp.where(first, nk[0:1], nk[1:2]), jnp.where(first, nv[0:1], nv[1:2]), rvalid
        )
        ros[2 * h] = o[0:16]
        ros[2 * h + 1] = o[16:32]

    def resident_all():
        l_kv().wait()
        over(N_TP - 1, lambda k: d_rq(tp_peer(k), tp_peer(k)).wait_recv())
        over(KVH, resident)
        over(N_TP - 1, lambda k: d_ro(tp_peer(k), i).start())
        rob[i] = ros[i]

    hvalid = iota((256, 256), 0) % 16 == iota((256, 256), 1) // 16

    def handed(p):
        h = head(p)
        over(N_GRP - 1, lambda k: d_kv_y(h, grp_peer(k), grp_peer(k)).wait_recv())
        for t2 in range(2):
            @pl.when(2 * h + t2 != i)
            def _():
                d_q(2 * h + t2, 2 * h + t2).wait_recv()
        q = jnp.concatenate(
            [
                qb[2 * h + t2, :, :, 128 * j:128 * j + 128].reshape(16, 128)
                for t2 in range(2) for j in range(8)
            ],
            axis=0,
        )
        k = kvb[h, :, :, 0:128].reshape(256, 128)
        v = kvb[h, :, :, 128:256].reshape(256, 128)
        kcols = pl.ds(pl.multiple_of(h * 128, 128), 128)
        vcols = pl.ds(pl.multiple_of(KVH * HD + h * 128, 128), 128)
        nk = nb[:, :, kcols].reshape(16, 128).astype(F32)
        nv = nb[:, :, vcols].reshape(16, 128).astype(F32)
        o = attend(q, k, v, jnp.tile(nk, (16, 1)), jnp.tile(nv, (16, 1)), hvalid)
        for t2 in range(2):
            for j in range(8):
                at = 16 * (8 * t2 + j)
                osd[2 * h + t2, :, :, 128 * j:128 * j + 128] = o[at:at + 16].reshape(8, 2, 128)
        for t2 in range(2):
            @pl.when(2 * h + t2 != i)
            def _():
                d_out(2 * h + t2, i).start()

    span(0, LAG, pack)
    pack_new()
    resident_all()
    over(N_GRP - 1, lambda k: d_new_y(grp_peer(k), grp_peer(k)).wait_recv())
    l_q().wait()

    def both(p):
        pack(p)
        handed(p - LAG)

    span(LAG, KVH, both)
    span(KVH - LAG, KVH, handed)
    l_out().start()

    over(N_TP - 1, lambda k: d_ro(tp_peer(k), tp_peer(k)).wait_recv())
    rof[...] = rob[...].reshape(256, 128).astype(F32)
    for j in range(8):
        for r in range(2):
            rot[pl.ds(32 * j + r, 16, stride=2), :] = rof[pl.ds(2 * j + r, 16, stride=16), :]
    for j in range(8):
        ro_ref[:, 128 * j:128 * j + 128] = rot[32 * j:32 * j + 32].astype(BF)

    d_place().wait_send()
    d_new().wait_send()

    def end_chunk(c):
        for part in range(2):
            d_stage1(c, part).wait_send()
        over(N_GRP - 1, lambda k: d_kv_y(c, grp_peer(k), g).wait_send())

    over(KVH, end_chunk)
    over(N_GRP - 1, lambda k: d_new_y(grp_peer(k), g).wait_send())

    def end_tp(k):
        t = tp_peer(k)
        d_rq(t, i).wait_send()
        d_q(t, i).wait_send()
        d_ro(t, i).wait_send()
        d_out(t, i).wait_send()
        d_out(t, t).wait_recv()

    over(N_TP - 1, end_tp)
    l_out().wait()


def write_kernel(ro, ho, kvb, ro_o, ho_o, hc_o, sems):
    copies = [
        pltpu.make_async_copy(ro, ro_o, sems.at[0]),
        pltpu.make_async_copy(ho, ho_o, sems.at[1]),
    ]
    for h in range(KVH):
        for part in range(2):
            copies.append(pltpu.make_async_copy(
                kvb.at[h, :, :, pl.ds(part * HD, HD)],
                hc_o.at[:, :, pl.ds((part * KVH + h) * HD, HD)],
                sems.at[2 + 2 * h + part],
            ))
    for copy in copies:
        copy.start()
    for copy in copies:
        copy.wait()


def body(
    resident_kv, resident_query, resident_new, lengths, fresh_kv, handed_query, fresh_new, matching
):
    vm = pl.BlockSpec(memory_space=pltpu.VMEM)
    hbm = pl.BlockSpec(memory_space=pltpu.HBM)
    dma = pltpu.SemaphoreType.DMA
    results = (
        jax.ShapeDtypeStruct((32, 1024), BF),
        jax.ShapeDtypeStruct((16, 8, 2, 1024), BF),
    )
    ro, ho, kvb = pl.pallas_call(
        kernel,
        out_shape=results + (jax.ShapeDtypeStruct((KVH, 8, 32, 2 * HD), BF),),
        in_specs=[hbm] * 8,
        out_specs=(vm, vm, vm),
        scratch_shapes=[
            pltpu.VMEM((32, 1024), BF),
            pltpu.VMEM((2, 2048), BF),
            pltpu.SMEM((2,), jnp.int32),
            pltpu.VMEM((8, 2048), BF),
            pltpu.VMEM((1, 8), jnp.int32),
            pltpu.VMEM((2, 256, 2048), BF),
            pltpu.VMEM((256, 128), F32),
            pltpu.VMEM((256, 128), F32),
            pltpu.VMEM((16, 16, 128), BF),
            pltpu.VMEM((16, 16, 128), BF),
            pltpu.VMEM((16, 16, 128), BF),
            pltpu.VMEM((16, 16, 128), BF),
            pltpu.VMEM((256, 128), F32),
            pltpu.VMEM((256, 128), F32),
            pltpu.VMEM((8, 128), jnp.int32),
            pltpu.VMEM((8, 128), jnp.int32),
            pltpu.VMEM((16, 2048), BF),
            pltpu.VMEM((16, 2048), BF),
            pltpu.VMEM((8, 2, 2048), BF),
            pltpu.VMEM((8, 2, 2048), BF),
            pltpu.VMEM((KVH, 8, 16, 2 * HD), BF),
            pltpu.VMEM((256, 128), BF),
            pltpu.VMEM((KVH, 8, 32, 2 * HD), BF),
            pltpu.VMEM((16, 8, 2, 1024), BF),
            pltpu.VMEM((16, 8, 2, 1024), BF),
            dma((8,)),
            dma, dma, dma, dma,
            dma((KVH, 2)), dma((KVH, 2)),
            dma((8,)), dma((8,)),
            dma((KVH, 8)), dma((KVH, 8)),
            dma((16,)), dma((16,)), dma((16,)), dma((16,)),
            dma((16,)), dma((16,)), dma((16,)), dma((16,)),
        ],
        compiler_params=pltpu.CompilerParams(
            collective_id=0, has_side_effects=True, vmem_limit_bytes=40 * 1024 * 1024
        ),
        name="handoff",
    )(*(
        pltpu.with_memory_space_constraint(array, pltpu.HBM)
        for array in (
            resident_kv, resident_query, resident_new, lengths, fresh_kv,
            handed_query.reshape(16, 8, 2, 1024), fresh_new, matching.reshape(1, 8),
        )
    ))
    ro, ho, hc = pl.pallas_call(
        write_kernel,
        out_shape=results + (jax.ShapeDtypeStruct((8, 32, 2048), BF),),
        in_specs=[vm] * 3,
        out_specs=(hbm, hbm, hbm),
        scratch_shapes=[dma((2 + 2 * KVH,))],
        compiler_params=pltpu.CompilerParams(vmem_limit_bytes=4 * 1024 * 1024),
        name="write",
    )(*(pltpu.with_memory_space_constraint(array, pltpu.VMEM) for array in (ro, ho, kvb)))
    return (
        ro,
        ho.reshape(1, 16, 8, 2, 1024),
        hc.reshape(1, 1, 8, 2, 16, 2048),
    )


def solution(mesh):
    return jax.shard_map(
        body,
        mesh=mesh,
        in_specs=(
            P(("side", "grp", "tp"), None, None),
            P(("side", "grp"), "tp"),
            P(("side", "grp", "tp"), None),
            P(("side", "grp", "tp")),
            P(("side", "grp", "tp"), None, None),
            P(("side", "grp"), None, None, None, "tp"),
            P(("side", "grp", "tp"), None),
            P(("side", "grp", "tp"), None),
        ),
        out_specs=(
            P(("side", "grp"), "tp"),
            P(("side", "grp"), None, None, None, "tp"),
            P(("side", "grp"), "tp", None, None, None, None),
        ),
        check_vma=False,
    )
```

time: 77.4 us -> 61.8 us (0.80)
  local copies, waits for them, and re-layouts: 9.74 us -> 0 us
  Pallas kernels: 66.6 us -> 61.1 us
    unnamed x18 -> x0, local copies, waits for them, and re-layouts: 9.74 us -> none
    pallas_call x1 -> x2, Pallas kernels: 66.6 us -> 61.1 us  [the longest x1 59.8 us: body(): pl.pallas_call(kernel, out_shape=results + (jax.ShapeDtypeStruct((KVH, 8,...]
where the time goes in v2:
time: 61.8 us; the launch traced here: 61.7 us
  Pallas kernels  61.1 us (99%)
  between operations  0.64 us (1%)
    pallas_call x1, Pallas kernels, body(): pl.pallas_call(kernel, out_shape=results + (jax.ShapeDtypeStruct((KVH, 8,...  59.8 us
    pallas_call x1, Pallas kernels, body(): pl.pallas_call(write_kernel, out_shape=results + (jax.ShapeDtypeStruct((8...  1.3 us

profile of v2, /device:TPU:1, one launch (start us, length us, event | category | flops | bytes accessed | tf_op | source)
XLA Modules:
  0.0 61.7 jit_solution(1737835366784770150)
XLA Ops:
  0.6 59.8 %handoff.1 = (bf16[32,1024]{1,0:T(8,128)(2,1)S(1)}, bf16[16,8,2,1024]{3,2,1,0:T(2,128)(2,1)S(1)}, bf16[8,8,32,256]{3,2,1,0:T(8,128)(2,1)S(1)}) custom-call(bf16[2,256,2048]{2,1,0:T(8,128)(2,1)} %kv_any.1, bf16[32,1024]{1,0:T(8,128)(2,1)} %rq_any.1, bf16[2,2048]{1,0:T(2,128)(2,1)} %rn_any.1, s32[2]{0:T(128)} %len_any.1, bf16[8,16,2048]{2,1,0:T(8,128)(2,1)} %fkv_any.1, ...), custom_call_target="tpu_custom_call" | custom-call | tf_op jit(solution)/shard_map/handoff/pallas_call | solution.py:349
  60.4 1.3 %write.1 = (bf16[32,1024]{1,0:T(8,128)(2,1)}, bf16[16,8,2,1024]{3,2,1,0:T(2,128)(2,1)}, bf16[8,32,2048]{2,1,0:T(8,128)(2,1)}) custom-call(bf16[32,1024]{1,0:T(8,128)(2,1)S(1)} %get-tuple-element.9.ro, bf16[16,8,2,1024]{3,2,1,0:T(2,128)(2,1)S(1)} %get-tuple-element.10.ho, bf16[8,8,32,256]{3,2,1,0:T(8,128)(2,1)S(1)} %get-tuple-element.11.kvb), custom_call_target="tpu_custom_call" | custom-call | tf_op jit(solution)/shard_map/write/pallas_call | solution.py:399

commit v3 on v2

--- a/solution.py
+++ b/solution.py
@@ -16,9 +16,10 @@
 N_TP = 16
 NEG_FILL = -1e30
 SCALE = 1.0 / math.sqrt(HD)
-LAG = 2
-FIRST = "kkqkqkqkqkkk"
-LAST = "kkkkkqkqkqkq"
+LAG = 3
+AHEAD = 4
+RESIDENT_AT = 5
+Q_FROM = 0
 
 
 def iota(shape, dim):
@@ -88,22 +89,34 @@
         return remote(new_s, new_r, nws, nwr, side=sp)
 
     def d_new_y(d, me):
-        return remote(npk.at[d], nb.at[me], nys.at[d], nyr.at[me], grp=d)
+        return remote(npk.at[d], nb.at[me], nys, nyr, grp=d)
 
     def d_kv_y(c, d, me):
-        return remote(pk.at[c, d], kvb.at[c, me], s2s.at[c, d], s2r.at[c, me], grp=d)
+        return remote(pk.at[c, d], kvb.at[c, me], s2s, s2r.at[c], grp=d)
 
     def d_rq(t, me):
-        return remote(rqs.at[t], rqb.at[me], rqss.at[t], rqr.at[me], tp=t)
+        return remote(rqs.at[t], rqb.at[me], rqss, rqr, tp=t)
 
     def d_q(t, me):
-        return remote(hq_any.at[t], qb.at[me], qs.at[t], qr.at[me], tp=t)
+        return remote(hq_any.at[t], qb.at[me], qs, qr.at[me], tp=t)
 
     def d_ro(t, me):
-        return remote(ros.at[t], rob.at[me], rosm.at[t], ror.at[me], tp=t)
+        return remote(ros.at[t], rob.at[me], rosm, ror, tp=t)
 
     def d_out(t, me):
-        return remote(osd.at[t], ho_ref.at[me], os_.at[t], orr.at[me], tp=t)
+        return remote(osd.at[t], ho_ref.at[me], os_, orr, tp=t)
+
+    def all_new_y():
+        return remote(npk.at[pl.ds(0, 7)], nb.at[pl.ds(0, 7)], nys, nyr, grp=g)
+
+    def all_kv_y(c):
+        return remote(pk.at[c, pl.ds(0, 7)], kvb.at[c, pl.ds(0, 7)], s2s, s2r.at[c], grp=g)
+
+    def all_kv_sent():
+        return remote(pk.at[pl.ds(0, 7)], kvb.at[pl.ds(0, 7)], s2s, s2r.at[0], grp=g)
+
+    def all_tp(src, dst, ss, rs):
+        return remote(src.at[pl.ds(0, 15)], dst.at[pl.ds(0, 15)], ss, rs, tp=i)
 
     def local(src, dst, at):
         return pltpu.make_async_copy(src, dst, loc.at[at])
@@ -138,6 +151,23 @@
         copy.start()
     l_q().start()
     l_kv().start()
+    def start1(p):
+        d_stage1(head(p), 0).start()
+        d_stage1(head(p), 1).start()
+
+    def start_q(n):
+        def one(dz):
+            t = (x + 4 - n) % 4 * 4 + (zh + dz) % 4
+
+            @pl.when(t != i)
+            def _():
+                d_q(t, i).start()
+
+        over(4, one)
+
+    pl.semaphore_wait(barrier, N_TP + N_GRP - 1)
+
+    span(0, AHEAD, start1)
     for copy in small:
         copy.wait()
 
@@ -164,34 +194,9 @@
     rqs[...] = rqt[...].astype(BF).reshape(16, 16, 128)
     rqb[i] = rqs[i]
 
-    pl.semaphore_wait(barrier, N_TP + N_GRP - 1)
-
-    def send_all(turns):
-        k = q = 0
-        for turn in turns:
-            if turn == "k":
-                d_stage1(head(k), 0).start()
-                d_stage1(head(k), 1).start()
-                k += 1
-            else:
-                for dz in range(4):
-                    if q or dz:
-                        d_q((x + 4 - q) % 4 * 4 + (zh + dz) % 4, i).start()
-                q += 1
-            if k == 1 and q == 0:
-                over(N_TP - 1, lambda n: d_rq(tp_peer(n), i).start())
-
     d_place().start()
     d_new().start()
-
-    @pl.when(zh < 2)
-    def _():
-        send_all(FIRST)
-
-    @pl.when(zh >= 2)
-    def _():
-        send_all(LAST)
-
+    over(N_TP - 1, lambda n: d_rq(tp_peer(n), i).start())
     d_place().wait_recv()
     sel[...] = jnp.where(iota((256, 128), 0) == place_r[0:1, :], 1.0, 0.0).astype(BF)
     sel16 = jnp.where(iota((16, 16), 0) == place_r[4:5, 0:16], 1.0, 0.0).astype(BF)
@@ -205,6 +210,14 @@
         pk[h] = y.reshape(8, 32, 2 * HD)
         over(N_GRP - 1, lambda k: d_kv_y(h, grp_peer(k), g).start())
         kvb[h, g] = pk[h, g]
+
+        @pl.when(p + AHEAD < KVH)
+        def _():
+            start1(p + AHEAD)
+
+        @pl.when((p >= Q_FROM) & (p < Q_FROM + 4))
+        def _():
+            start_q(p - Q_FROM)
 
     def pack_new():
         d_new().wait_recv()
@@ -236,7 +249,7 @@
 
     def resident_all():
         l_kv().wait()
-        over(N_TP - 1, lambda k: d_rq(tp_peer(k), tp_peer(k)).wait_recv())
+        all_tp(rqs, rqb, rqss, rqr).wait_recv()
         over(KVH, resident)
         over(N_TP - 1, lambda k: d_ro(tp_peer(k), i).start())
         rob[i] = ros[i]
@@ -245,7 +258,7 @@
 
     def handed(p):
         h = head(p)
-        over(N_GRP - 1, lambda k: d_kv_y(h, grp_peer(k), grp_peer(k)).wait_recv())
+        all_kv_y(h).wait_recv()
         for t2 in range(2):
             @pl.when(2 * h + t2 != i)
             def _():
@@ -275,19 +288,20 @@
 
     span(0, LAG, pack)
     pack_new()
-    resident_all()
-    over(N_GRP - 1, lambda k: d_new_y(grp_peer(k), grp_peer(k)).wait_recv())
+    all_new_y().wait_recv()
     l_q().wait()
 
     def both(p):
         pack(p)
         handed(p - LAG)
 
-    span(LAG, KVH, both)
+    span(LAG, RESIDENT_AT, both)
+    resident_all()
+    span(RESIDENT_AT, KVH, both)
     span(KVH - LAG, KVH, handed)
     l_out().start()
 
-    over(N_TP - 1, lambda k: d_ro(tp_peer(k), tp_peer(k)).wait_recv())
+    all_tp(ros, rob, rosm, ror).wait_recv()
     rof[...] = rob[...].reshape(256, 128).astype(F32)
     for j in range(8):
         for r in range(2):
@@ -298,23 +312,18 @@
     d_place().wait_send()
     d_new().wait_send()
 
-    def end_chunk(c):
-        for part in range(2):
-            d_stage1(c, part).wait_send()
-        over(N_GRP - 1, lambda k: d_kv_y(c, grp_peer(k), g).wait_send())
-
-    over(KVH, end_chunk)
-    over(N_GRP - 1, lambda k: d_new_y(grp_peer(k), g).wait_send())
-
-    def end_tp(k):
-        t = tp_peer(k)
-        d_rq(t, i).wait_send()
-        d_q(t, i).wait_send()
-        d_ro(t, i).wait_send()
-        d_out(t, i).wait_send()
-        d_out(t, t).wait_recv()
-
-    over(N_TP - 1, end_tp)
+    def end_kv(h):
+        d_stage1(h, 0).wait_send()
+        d_stage1(h, 1).wait_send()
+
+    over(KVH, end_kv)
+    all_kv_sent().wait_send()
+    all_new_y().wait_send()
+    all_tp(rqs, rqb, rqss, rqr).wait_send()
+    all_tp(hq_any, qb, qs, qr.at[i]).wait_send()
+    all_tp(ros, rob, rosm, ror).wait_send()
+    all_tp(osd, ho_ref, os_, orr).wait_send()
+    all_tp(osd, ho_ref, os_, orr).wait_recv()
     l_out().wait()
 
 
@@ -380,10 +389,10 @@
             dma((8,)),
             dma, dma, dma, dma,
             dma((KVH, 2)), dma((KVH, 2)),
-            dma((8,)), dma((8,)),
-            dma((KVH, 8)), dma((KVH, 8)),
-            dma((16,)), dma((16,)), dma((16,)), dma((16,)),
-            dma((16,)), dma((16,)), dma((16,)), dma((16,)),
+            dma, dma,
+            dma, dma((KVH,)),
+            dma, dma, dma, dma((16,)),
+            dma, dma, dma, dma,
         ],
         compiler_params=pltpu.CompilerParams(
             collective_id=0, has_side_effects=True, vmem_limit_bytes=40 * 1024 * 1024

time: 61.8 us -> 58.7 us (0.950)
  Pallas kernels: 61.1 us -> 57.6 us
    pallas_call x1, Pallas kernels: 59.8 us -> 56.3 us  [body(): pl.pallas_call(kernel, out_shape=results + (jax.ShapeDtypeStruct((KVH, 8,...]
where the time goes in v3:
time: 58.7 us; the launch traced here: 58.2 us
  Pallas kernels  57.6 us (98%)
  between operations  0.64 us (1%)
    pallas_call x1, Pallas kernels, body(): pl.pallas_call(kernel, out_shape=results + (jax.ShapeDtypeStruct((KVH, 8,...  56.3 us
    pallas_call x1, Pallas kernels, body(): pl.pallas_call(write_kernel, out_shape=results + (jax.ShapeDtypeStruct((8...  1.3 us

profile of v3, /device:TPU:1, one launch (start us, length us, event | category | flops | bytes accessed | tf_op | source)
XLA Modules:
  0.0 58.2 jit_solution(13796468160809689027)
XLA Ops:
  0.6 56.3 %handoff.1 = (bf16[32,1024]{1,0:T(8,128)(2,1)S(1)}, bf16[16,8,2,1024]{3,2,1,0:T(2,128)(2,1)S(1)}, bf16[8,8,32,256]{3,2,1,0:T(8,128)(2,1)S(1)}) custom-call(bf16[2,256,2048]{2,1,0:T(8,128)(2,1)} %kv_any.1, bf16[32,1024]{1,0:T(8,128)(2,1)} %rq_any.1, bf16[2,2048]{1,0:T(2,128)(2,1)} %rn_any.1, s32[2]{0:T(128)} %len_any.1, bf16[8,16,2048]{2,1,0:T(8,128)(2,1)} %fkv_any.1, ...), custom_call_target="tpu_custom_call" | custom-call | tf_op jit(solution)/shard_map/handoff/pallas_call | solution.py:358
  56.9 1.3 %write.1 = (bf16[32,1024]{1,0:T(8,128)(2,1)}, bf16[16,8,2,1024]{3,2,1,0:T(2,128)(2,1)}, bf16[8,32,2048]{2,1,0:T(8,128)(2,1)}) custom-call(bf16[32,1024]{1,0:T(8,128)(2,1)S(1)} %get-tuple-element.9.ro, bf16[16,8,2,1024]{3,2,1,0:T(2,128)(2,1)S(1)} %get-tuple-element.10.ho, bf16[8,8,32,256]{3,2,1,0:T(8,128)(2,1)S(1)} %get-tuple-element.11.kvb), custom_call_target="tpu_custom_call" | custom-call | tf_op jit(solution)/shard_map/write/pallas_call | solution.py:408

commit v4 on v3

--- a/solution.py
+++ b/solution.py
@@ -54,7 +54,10 @@
     x, zh = i // 4, i % 4
 
     def head(p):
-        return 2 * ((x + p) % 4) + p // 4
+        alternate = side % 2
+        step = p + alternate * (p // 2 - p)
+        odd = p // 4 + alternate * (p % 2 - p // 4)
+        return 2 * ((x + step) % 4) + odd
 
     def remote(src, dst, ss, rs, **dev):
         return pltpu.make_async_remote_copy(
@@ -185,7 +188,9 @@
     wide = places(lane // 16) * 16 + lane % 16
     narrow = jnp.where(lane < 8, places(lane), -1)
     place_s[...] = jnp.where(row < 4, wide, narrow)
-    new_s[...] = jnp.concatenate([fn_v[...], jnp.zeros((8, 2 * KVH * HD), BF)], axis=0)
+    new_s[...] = jnp.concatenate(
+        [fn_v[:, 128 * c:128 * c + 128].astype(F32) for c in range(16)], axis=0
+    ).astype(BF)
     for j in range(8):
         rqf[32 * j:32 * j + 32] = rq_v[:, 128 * j:128 * j + 128].astype(F32)
     for j in range(8):
@@ -199,7 +204,7 @@
     over(N_TP - 1, lambda n: d_rq(tp_peer(n), i).start())
     d_place().wait_recv()
     sel[...] = jnp.where(iota((256, 128), 0) == place_r[0:1, :], 1.0, 0.0).astype(BF)
-    sel16 = jnp.where(iota((16, 16), 0) == place_r[4:5, 0:16], 1.0, 0.0).astype(BF)
+    sel16 = jnp.where(iota((16, 8), 0) == place_r[4:5, 0:8], 1.0, 0.0)
 
     def pack(p):
         h = head(p)
@@ -221,9 +226,10 @@
 
     def pack_new():
         d_new().wait_recv()
+        new = new_r[...].astype(F32)
         for c in range(16):
             cols = slice(128 * c, 128 * c + 128)
-            y = jnp.dot(sel16, new_r[:, cols], preferred_element_type=F32).astype(BF)
+            y = jnp.dot(sel16, new[8 * c:8 * c + 8], preferred_element_type=F32).astype(BF)
             npk[:, :, cols] = y.reshape(8, 2, 128)
         over(N_GRP - 1, lambda k: d_new_y(grp_peer(k), g).start())
         nb[g] = npk[g]
@@ -377,8 +383,8 @@
             pltpu.VMEM((256, 128), F32),
             pltpu.VMEM((8, 128), jnp.int32),
             pltpu.VMEM((8, 128), jnp.int32),
-            pltpu.VMEM((16, 2048), BF),
-            pltpu.VMEM((16, 2048), BF),
+            pltpu.VMEM((128, 128), BF),
+            pltpu.VMEM((128, 128), BF),
             pltpu.VMEM((8, 2, 2048), BF),
             pltpu.VMEM((8, 2, 2048), BF),
             pltpu.VMEM((KVH, 8, 16, 2 * HD), BF),

time: 58.7 us -> 57.3 us (0.976)
  the two profiles are of different devices: /device:TPU:1 before, /device:TPU:64 now
where the time goes in v4:
time: 57.3 us; the launch traced here: 57.1 us
  Pallas kernels  56.5 us (99%)
  between operations  0.64 us (1%)
    pallas_call x1, Pallas kernels, body(): pl.pallas_call(kernel, out_shape=results + (jax.ShapeDtypeStruct((KVH, 8,...  55.2 us
    pallas_call x1, Pallas kernels, body(): pl.pallas_call(write_kernel, out_shape=results + (jax.ShapeDtypeStruct((8...  1.3 us

profile of v4, /device:TPU:64, one launch (start us, length us, event | category | flops | bytes accessed | tf_op | source)
XLA Modules:
  0.0 57.1 jit_solution(18207488363344506543)
XLA Ops:
  0.6 55.2 %handoff.1 = (bf16[32,1024]{1,0:T(8,128)(2,1)S(1)}, bf16[16,8,2,1024]{3,2,1,0:T(2,128)(2,1)S(1)}, bf16[8,8,32,256]{3,2,1,0:T(8,128)(2,1)S(1)}) custom-call(bf16[2,256,2048]{2,1,0:T(8,128)(2,1)} %kv_any.1, bf16[32,1024]{1,0:T(8,128)(2,1)} %rq_any.1, bf16[2,2048]{1,0:T(2,128)(2,1)} %rn_any.1, s32[2]{0:T(128)} %len_any.1, bf16[8,16,2048]{2,1,0:T(8,128)(2,1)} %fkv_any.1, ...), custom_call_target="tpu_custom_call" | custom-call | tf_op jit(solution)/shard_map/handoff/pallas_call | solution.py:364
  55.8 1.3 %write.1 = (bf16[32,1024]{1,0:T(8,128)(2,1)}, bf16[16,8,2,1024]{3,2,1,0:T(2,128)(2,1)}, bf16[8,32,2048]{2,1,0:T(8,128)(2,1)}) custom-call(bf16[32,1024]{1,0:T(8,128)(2,1)S(1)} %get-tuple-element.9.ro, bf16[16,8,2,1024]{3,2,1,0:T(2,128)(2,1)S(1)} %get-tuple-element.10.ho, bf16[8,8,32,256]{3,2,1,0:T(8,128)(2,1)S(1)} %get-tuple-element.11.kvb), custom_call_target="tpu_custom_call" | custom-call | tf_op jit(solution)/shard_map/write/pallas_call | solution.py:414

commit v5 on v4

--- a/solution.py
+++ b/solution.py
@@ -188,9 +188,11 @@
     wide = places(lane // 16) * 16 + lane % 16
     narrow = jnp.where(lane < 8, places(lane), -1)
     place_s[...] = jnp.where(row < 4, wide, narrow)
+    d_place().start()
     new_s[...] = jnp.concatenate(
         [fn_v[:, 128 * c:128 * c + 128].astype(F32) for c in range(16)], axis=0
     ).astype(BF)
+    d_new().start()
     for j in range(8):
         rqf[32 * j:32 * j + 32] = rq_v[:, 128 * j:128 * j + 128].astype(F32)
     for j in range(8):
@@ -199,8 +201,6 @@
     rqs[...] = rqt[...].astype(BF).reshape(16, 16, 128)
     rqb[i] = rqs[i]
 
-    d_place().start()
-    d_new().start()
     over(N_TP - 1, lambda n: d_rq(tp_peer(n), i).start())
     d_place().wait_recv()
     sel[...] = jnp.where(iota((256, 128), 0) == place_r[0:1, :], 1.0, 0.0).astype(BF)

time: 57.3 us -> 57.3 us (level)
  no operation moved by 1% of the time
where the time goes in v5:
time: 57.3 us; the launch traced here: 57.2 us
  Pallas kernels  56.6 us (99%)
  between operations  0.64 us (1%)
    pallas_call x1, Pallas kernels, body(): pl.pallas_call(kernel, out_shape=results + (jax.ShapeDtypeStruct((KVH, 8,...  55.3 us
    pallas_call x1, Pallas kernels, body(): pl.pallas_call(write_kernel, out_shape=results + (jax.ShapeDtypeStruct((8...  1.3 us

profile of v5, /device:TPU:64, one launch (start us, length us, event | category | flops | bytes accessed | tf_op | source)
XLA Modules:
  0.0 57.2 jit_solution(11734492693369854285)
XLA Ops:
  0.6 55.3 %handoff.1 = (bf16[32,1024]{1,0:T(8,128)(2,1)S(1)}, bf16[16,8,2,1024]{3,2,1,0:T(2,128)(2,1)S(1)}, bf16[8,8,32,256]{3,2,1,0:T(8,128)(2,1)S(1)}) custom-call(bf16[2,256,2048]{2,1,0:T(8,128)(2,1)} %kv_any.1, bf16[32,1024]{1,0:T(8,128)(2,1)} %rq_any.1, bf16[2,2048]{1,0:T(2,128)(2,1)} %rn_any.1, s32[2]{0:T(128)} %len_any.1, bf16[8,16,2048]{2,1,0:T(8,128)(2,1)} %fkv_any.1, ...), custom_call_target="tpu_custom_call" | custom-call | tf_op jit(solution)/shard_map/handoff/pallas_call | solution.py:364
  55.9 1.3 %write.1 = (bf16[32,1024]{1,0:T(8,128)(2,1)}, bf16[16,8,2,1024]{3,2,1,0:T(2,128)(2,1)}, bf16[8,32,2048]{2,1,0:T(8,128)(2,1)}) custom-call(bf16[32,1024]{1,0:T(8,128)(2,1)S(1)} %get-tuple-element.9.ro, bf16[16,8,2,1024]{3,2,1,0:T(2,128)(2,1)S(1)} %get-tuple-element.10.ho, bf16[8,8,32,256]{3,2,1,0:T(8,128)(2,1)S(1)} %get-tuple-element.11.kvb), custom_call_target="tpu_custom_call" | custom-call | tf_op jit(solution)/shard_map/write/pallas_call | solution.py:414
